TPU v7x, 256 devices: a whole 4x4x8 slice. The times are simulated.
256 devices in a mesh: row: 16 (over z, core), col: 4 (over y), rep: 4 (over x).
Axes of the slice: x: 4, y: 4, z: 8, core: 2. Of those that a mesh axis runs over, the one named last changes fastest.
Arguments:
- density: bfloat16 [8192, 8192], P('row', 'col'), may hold values from -1.5 to 1.75, as said below
- pattern_density: int32 [256, 256], P('row', 'col'), may hold values 0 or 1
- pattern_square: int32 [256, 256], P('row', 'col'), may hold values 0 or 1
- pattern_cube: int32 [256, 256], P('row', 'col'), may hold values 0 or 1
Outputs:
- purified: bfloat16 [8192, 8192], P('row', ('col', 'rep'))
Inputs may be any that keep to these rules, and one draw needn't show every extreme that they name: `density`: symmetric.
All inputs are finite; a program needn't handle non-finite values. No bound on the sum of `pattern_density` or of `pattern_square` or of `pattern_cube` on one device may be relied on, other than what follows from the above.
Results may differ from a plain program's by a relative error of at most 0.0054.
Values may be sent and summed in bfloat16 or wider, within the bound.
No kernel may reach another device: no remote copies, remote signals or barrier semaphores. Data moves between devices by JAX's collectives and lax.ppermute only.
A program may use at most 64 MiB of HBM per device.

v0:
```python
import jax
import jax.numpy as jnp
from jax import lax
from jax.sharding import PartitionSpec as P

BLK = 32


def spread(pattern, block_width):
    blocks_down, blocks_across = pattern.shape
    wide = jnp.broadcast_to(
        pattern[:, None, :, None] > 0, (blocks_down, block_width, blocks_across, block_width)
    )
    return wide.reshape(blocks_down * block_width, blocks_across * block_width)


def column_share(matrix, rep_depth, rep_layer, block_width):
    tile_rows, tile_width = matrix.shape
    shaped = matrix.reshape(
        tile_rows, tile_width // (rep_depth * block_width), rep_depth, block_width
    )
    picked = lax.dynamic_index_in_dim(shaped, rep_layer, 2, keepdims=False)
    return picked.reshape(tile_rows, tile_width // rep_depth)


def row_share(matrix, rep_depth, rep_layer, block_width):
    tile_rows, tile_width = matrix.shape
    shaped = matrix.reshape(
        tile_rows // (rep_depth * block_width), rep_depth, block_width, tile_width
    )
    picked = lax.dynamic_index_in_dim(shaped, rep_layer, 1, keepdims=False)
    return picked.reshape(tile_rows // rep_depth, tile_width)


def body(density, pattern_density, pattern_square, pattern_cube):
    tile_rows, tile_width = density.shape
    rep_depth = lax.axis_size("rep")
    rep_layer = lax.axis_index("rep")
    share_width = tile_width // rep_depth
    share_start = rep_layer * share_width
    masked = jnp.where(spread(pattern_density, BLK), density, jnp.zeros_like(density))
    right_share = row_share(masked, rep_depth, rep_layer, BLK)
    left_band = lax.all_gather(
        column_share(masked, rep_depth, rep_layer, BLK), "col", axis=1, tiled=True
    )
    right_band = lax.all_gather(right_share, "row", axis=0, tiled=True)
    product_one = jnp.dot(left_band, right_band, preferred_element_type=jnp.float32)
    square_keep = spread(pattern_square, BLK)
    summed = lax.psum(product_one, "rep")
    square = jnp.where(square_keep, summed, jnp.float32(0.0)).astype(jnp.bfloat16)
    left_square = lax.all_gather(
        column_share(square, rep_depth, rep_layer, BLK), "col", axis=1, tiled=True
    )
    product_two = jnp.dot(left_square, right_band, preferred_element_type=jnp.float32)
    cube_share = lax.psum_scatter(product_two, "rep", scatter_dimension=1, tiled=True)
    cube_keep = lax.dynamic_slice_in_dim(spread(pattern_cube, BLK), share_start, share_width, 1)
    square_cols = lax.dynamic_slice_in_dim(square, share_start, share_width, 1).astype(jnp.float32)
    cube = jnp.where(cube_keep, cube_share, jnp.float32(0.0))
    return (3.0 * square_cols - 2.0 * cube).astype(jnp.bfloat16)


def solution(mesh):
    placed = (P("row", "col"), P("row", "col"), P("row", "col"), P("row", "col"))
    return jax.shard_map(
        body, mesh=mesh, in_specs=placed, out_specs=P("row", ("col", "rep")), check_vma=False
    )
```

profile of v0, /device:TPU:1, one launch (start us, length us, event | category | flops | bytes accessed | tf_op | source)
XLA Modules:
  0.0 318.8 jit_solution(17400307454804896158)
XLA Ops:
  6.5 0.7 broadcast_compare_fusion.1
  7.2 3.1 broadcast_in_dim.30
  10.3 10.4 %reshape.37 = pred[512,2048]{1,0:T(8,128)(4,1)S(1)} reshape(pred[16,32,64,32]{3,2,1,0:T(8,128)(4,1)} %broadcast_in_dim.30) | data formatting | bytes 2097152 | tf_op jit(solution)/shard_map/reshape | solution.py:14
  20.7 1.8 broadcast_select_fusion
  22.5 2.5 copy.5
  25.0 1.9 constant_dynamic-slice_fusion.2
  27.0 0.9 constant_dynamic-slice_fusion.1
  28.0 3.1 broadcast_in_dim.15
  31.1 10.4 %reshape.36 = pred[512,2048]{1,0:T(8,128)(4,1)S(1)} reshape(pred[16,32,64,32]{3,2,1,0:T(8,128)(4,1)} %broadcast_in_dim.15) | data formatting | bytes 2097152 | tf_op jit(solution)/shard_map/reshape | solution.py:14
  41.4 22.9 %all-gather.4.cloned.1.call-done = bf16[512,2048]{0,1:T(8,128)(2,1)} async-done(((bf16[512,512]{0,1:T(8,128)(2,1)}), bf16[512,2048]{0,1:T(8,128)(2,1)}) %all-gather.4.cloned.1.call-update) | async-done | bytes 2097168 | tf_op jit(solution)/shard_map/all_gather | solution.py:43
  64.3 58.2 %all-gather.6.cloned.1.call-done = bf16[2048,2048]{1,0:T(8,128)(2,1)} async-done(((bf16[128,2048]{1,0:T(8,128)(2,1)}), bf16[2048,2048]{1,0:T(8,128)(2,1)}) %all-gather.6.cloned.1.call-update) | async-done | bytes 8388624 | tf_op jit(solution)/shard_map/all_gather | solution.py:46
  122.5 10.5 %fusion = f32[512,2048]{1,0:T(8,128)} fusion(bf16[512,2048]{0,1:T(8,128)(2,1)} %all-gather.4.cloned.1.call-done, bf16[2048,2048]{1,0:T(8,128)(2,1)} %all-gather.6.cloned.1.call-done), kind=kOutput, calls=%fused_computation.9 | convolution fusion | flops 4294967296 | bytes 14680064 | tf_op jit(solution)/shard_map/dot_general | solution.py:47
  133.1 78.3 %all-reduce.1 = bf16[512,2048]{1,0:T(8,128)(2,1)} all-reduce(f32[512,2048]{1,0:T(8,128)} %fusion), channel_id=1, replica_groups=mesh['row'=16,'col'=4,'rep'=4] {'rep'}, use_global_device_ids=true, to_apply=%region_0.1 | all-reduce | flops 1048576 | bytes 6291456 | tf_op jit(solution)/shard_map/psum | solution.py:49
  211.4 2.3 select_convert_fusion
  213.7 2.6 copy.6
  216.3 1.9 constant_dynamic-slice_fusion
  218.2 0.2 reduce-scatter.2.cloned.1.call-start
  218.4 31.4 %all-gather.8.cloned.1.call-done = bf16[512,2048]{0,1:T(8,128)(2,1)} async-done(((bf16[512,512]{0,1:T(8,128)(2,1)}), bf16[512,2048]{0,1:T(8,128)(2,1)}) %all-gather.8.cloned.1.call-update) | async-done | bytes 2097168 | tf_op jit(solution)/shard_map/all_gather | solution.py:51
  249.8 10.5 %fusion.1 = f32[512,2048]{1,0:T(8,128)} fusion(bf16[512,2048]{0,1:T(8,128)(2,1)} %all-gather.8.cloned.1.call-done, bf16[2048,2048]{1,0:T(8,128)(2,1)} %all-gather.6.cloned.1.call-done), kind=kOutput, calls=%fused_computation.10 | convolution fusion | flops 4294967296 | bytes 14680064 | tf_op jit(solution)/shard_map/dot_general | solution.py:54
  260.3 0.7 copy-done.1
  261.0 3.1 broadcast_in_dim.33
  264.1 10.5 %reshape.42 = pred[512,2048]{1,0:T(8,128)(4,1)S(1)} reshape(pred[16,32,64,32]{3,2,1,0:T(8,128)(4,1)} %broadcast_in_dim.33) | data formatting | bytes 2097152 | tf_op jit(solution)/shard_map/reshape | solution.py:14
  274.6 35.3 %reduce-scatter.2.cloned.1.call-done = f32[512,512]{1,0:T(8,128)} async-done(((f32[512,2048]{1,0:T(8,128)}), f32[512,512]{1,0:T(8,128)}) %reduce-scatter.2.cloned.1.call-update) | async-done | bytes 1048592 | tf_op jit(solution)/shard_map/reduce_scatter | solution.py:55
  309.9 2.3 subtract_convert_fusion
  (12 shorter events, 0.2 us)
Async XLA Ops:
  6.5 57.8 %all-gather.4.cloned.1.call-start = ((), (), s32[]{:S(2)}) async-start(), calls=%async_computation.1 | async-start | bytes 2621440 | tf_op jit(solution)/shard_map/all_gather | solution.py:43
  25.0 2.9 copy-start
  27.0 95.6 %all-gather.6.cloned.1.call-start = ((), (), s32[]{:S(2)}) async-start(), calls=%async_computation.2 | async-start | bytes 8912896 | tf_op jit(solution)/shard_map/all_gather | solution.py:46
  27.9 221.9 %all-gather.8.cloned.1.call-start = ((), (), s32[]{:S(2)}) async-start(), calls=%async_computation.3 | async-start | bytes 2621440 | tf_op jit(solution)/shard_map/all_gather | solution.py:51
  218.2 91.7 %reduce-scatter.2.cloned.1.call-start = ((), (), s32[]{:S(2)}) async-start(), calls=%async_computation.4 | async-start | bytes 5242880 | tf_op jit(solution)/shard_map/reduce_scatter | solution.py:55
  260.3 0.7 copy-start.1
Sparse Core Ops, SparseCore 0:
  27.1 37.2 all-gather.3
  66.1 56.3 all-gather.5
  218.3 31.4 all-gather.7
  260.5 49.4 reduce-scatter.1
where the time goes:
time: 320 us; the launch traced here: 319 us
  waiting for transfers between devices  148 us (46%)
  blocking collectives  78.3 us (24%)
  local copies, waits for them, and re-layouts  50.9 us (16%)
  matrix products  21.1 us (7%)
  between operations  13.2 us (4%)
  other arithmetic  7.09 us (2%)
    psum x1, blocking collectives, body(): summed = lax.psum(product_one, 'rep')  78.3 us
    all_gather x1, waiting for transfers between devices, body(): right_band = lax.all_gather(right_share, 'row', axis=0, tiled=True)  58.2 us
    reduce_scatter x1, waiting for transfers between devices, body(): lax.psum_scatter(product_two, 'rep', scatter_dimension=1, tiled=True)  35.3 us
    all_gather x1, waiting for transfers between devices, body(): lax.all_gather(column_share(square, rep_depth, rep_layer, BLK), 'col', ax...  31.4 us
    reshape x3, local copies, waits for them, and re-layouts, spread(): return wide.reshape(blocks_down * block_width, blocks_across * block_width)  31.3 us
    all_gather x1, waiting for transfers between devices, body(): lax.all_gather(column_share(masked, rep_depth, rep_layer, BLK), 'col', ax...  22.9 us
    dot_general x1, matrix products, body(): jnp.dot(left_square, right_band, preferred_element_type=jnp.float32)  10.5 us
    dot_general x1, matrix products, body(): jnp.dot(left_band, right_band, preferred_element_type=jnp.float32)  10.5 us
  transfers between devices with their start and end apart: 4, of which 4 were waited for; matrix products, arithmetic and copies ran while one was open for 9% of the time, Pallas kernels for 0%

commit v1 on v0

--- a/solution.py
+++ b/solution.py
@@ -46,7 +46,9 @@
     right_band = lax.all_gather(right_share, "row", axis=0, tiled=True)
     product_one = jnp.dot(left_band, right_band, preferred_element_type=jnp.float32)
     square_keep = spread(pattern_square, BLK)
-    summed = lax.psum(product_one, "rep")
+    summed = product_one
+    for hop in (1, 2):
+        summed = summed + lax.ppermute(summed, "rep", [(dev, dev ^ hop) for dev in range(4)])
     square = jnp.where(square_keep, summed, jnp.float32(0.0)).astype(jnp.bfloat16)
     left_square = lax.all_gather(
         column_share(square, rep_depth, rep_layer, BLK), "col", axis=1, tiled=True

time: 320 us -> 431 us (1.35)
  waiting for transfers between devices: 148 us -> 331 us
  blocking collectives: 78.3 us -> 0 us
  other arithmetic: 7.09 us -> 12.3 us
    ppermute x0 -> x2, waiting for transfers between devices: none -> 167 us  [body(): lax.ppermute(summed, 'rep', [(dev, dev ^ hop) for dev in range(4)])]
    psum x1 -> x0, blocking collectives: 78.3 us -> none  [body(): summed = lax.psum(product_one, 'rep')]
    all_gather x1, waiting for transfers between devices: 22.9 us -> 36.4 us  [body(): lax.all_gather(column_share(masked, rep_depth, rep_layer, BLK), 'col', ax...]
  transfers between devices with their start and end apart: 4 -> 6, of which waited for: 4 -> 6; matrix products, arithmetic and copies ran while one was open for 9% -> 7% of each run, Pallas kernels for 0% -> 0%
where the time goes in v1:
time: 431 us; the launch traced here: 429 us
  waiting for transfers between devices  331 us (77%)
  local copies, waits for them, and re-layouts  51 us (12%)
  matrix products  18.1 us (4%)
  between operations  13.2 us (3%)
  other arithmetic  12.3 us (3%)
    ppermute x2, waiting for transfers between devices, body(): lax.ppermute(summed, 'rep', [(dev, dev ^ hop) for dev in range(4)])  167 us
    all_gather x1, waiting for transfers between devices, body(): right_band = lax.all_gather(right_share, 'row', axis=0, tiled=True)  58.2 us
    all_gather x1, waiting for transfers between devices, body(): lax.all_gather(column_share(masked, rep_depth, rep_layer, BLK), 'col', ax...  36.4 us
    reduce_scatter x1, waiting for transfers between devices, body(): lax.psum_scatter(product_two, 'rep', scatter_dimension=1, tiled=True)  35.3 us
    all_gather x1, waiting for transfers between devices, body(): lax.all_gather(column_share(square, rep_depth, rep_layer, BLK), 'col', ax...  33.2 us
    reshape x3, local copies, waits for them, and re-layouts, spread(): return wide.reshape(blocks_down * block_width, blocks_across * block_width)  31.3 us
    dot_general x1, matrix products, body(): jnp.dot(left_square, right_band, preferred_element_type=jnp.float32)  10.6 us
    broadcast_in_dim x3, local copies, waits for them, and re-layouts, spread(): jnp.broadcast_to(pattern[:, None, :, None] > 0, (blocks_down, block_width...  9.29 us
  transfers between devices with their start and end apart: 6, of which 6 were waited for; matrix products, arithmetic and copies ran while one was open for 7% of the time, Pallas kernels for 0%

profile of v1, /device:TPU:1, one launch (start us, length us, event | category | flops | bytes accessed | tf_op | source)
XLA Modules:
  0.0 429.4 jit_solution(4754047633265827870)
XLA Ops:
  7.2 3.1 broadcast_in_dim.30
  10.3 10.4 %reshape.37 = pred[512,2048]{1,0:T(8,128)(4,1)S(1)} reshape(pred[16,32,64,32]{3,2,1,0:T(8,128)(4,1)} %broadcast_in_dim.30) | data formatting | bytes 2097152 | tf_op jit(solution)/shard_map/reshape | solution.py:14
  20.7 1.8 broadcast_select_fusion
  22.5 2.5 copy.5
  25.1 1.9 constant_dynamic-slice_fusion.2
  27.9 36.4 %all-gather.4.cloned.1.call-done = bf16[512,2048]{0,1:T(8,128)(2,1)} async-done(((bf16[512,512]{0,1:T(8,128)(2,1)}), bf16[512,2048]{0,1:T(8,128)(2,1)}) %all-gather.4.cloned.1.call-update) | async-done | bytes 2097168 | tf_op jit(solution)/shard_map/all_gather | solution.py:43
  64.3 58.2 %all-gather.6.cloned.1.call-done = bf16[2048,2048]{1,0:T(8,128)(2,1)} async-done(((bf16[128,2048]{1,0:T(8,128)(2,1)}), bf16[2048,2048]{1,0:T(8,128)(2,1)}) %all-gather.6.cloned.1.call-update) | async-done | bytes 8388624 | tf_op jit(solution)/shard_map/all_gather | solution.py:46
  122.6 7.6 %fusion = f32[512,2048]{1,0:T(8,128)S(1)} fusion(bf16[512,2048]{0,1:T(8,128)(2,1)} %all-gather.4.cloned.1.call-done, bf16[2048,2048]{1,0:T(8,128)(2,1)} %all-gather.6.cloned.1.call-done), kind=kOutput, calls=%fused_computation.9 | convolution fusion | flops 4294967296 | bytes 14680064 | tf_op jit(solution)/shard_map/dot_general | solution.py:47
  130.2 1.3 collective-permute-start
  131.4 90.7 %collective-permute-done = f32[512,2048]{1,0:T(8,128)S(1)} collective-permute-done((f32[512,2048]{1,0:T(8,128)S(1)}, f32[512,2048]{1,0:T(8,128)S(1)}, u32[]{:S(2)}, u32[]{:S(2)}) %collective-permute-start) | collective-permute-done | bytes 4194336 | tf_op jit(solution)/shard_map/ppermute | solution.py:51
  222.2 2.7 add.20
  224.9 2.7 collective-permute-start.1
  227.6 3.1 broadcast_in_dim.15
  230.7 10.4 %reshape.36 = pred[512,2048]{1,0:T(8,128)(4,1)S(1)} reshape(pred[16,32,64,32]{3,2,1,0:T(8,128)(4,1)} %broadcast_in_dim.15) | data formatting | bytes 2097152 | tf_op jit(solution)/shard_map/reshape | solution.py:14
  241.1 76.6 %collective-permute-done.1 = f32[512,2048]{1,0:T(8,128)} collective-permute-done((f32[512,2048]{1,0:T(8,128)}, f32[512,2048]{1,0:T(8,128)}, u32[]{:S(2)}, u32[]{:S(2)}) %collective-permute-start.1) | collective-permute-done | bytes 4194336 | tf_op jit(solution)/shard_map/ppermute | solution.py:51
  317.7 4.7 %select_convert_fusion = bf16[512,2048]{1,0:T(8,128)(2,1)S(1)} fusion(pred[512,2048]{1,0:T(8,128)(4,1)S(1)} %reshape.36, f32[512,2048]{1,0:T(8,128)} %add.20, f32[512,2048]{1,0:T(8,128)} %collective-permute-done.1), kind=kLoop, calls=%fused_computation | loop fusion | flops 3145728 | bytes 11534336 | tf_op jit(solution)/shard_map/convert_element_type | solution.py:52
  322.4 2.6 copy.6
  325.0 1.9 constant_dynamic-slice_fusion
  327.2 33.2 %all-gather.8.cloned.1.call-done = bf16[512,2048]{0,1:T(8,128)(2,1)} async-done(((bf16[512,512]{0,1:T(8,128)(2,1)}), bf16[512,2048]{0,1:T(8,128)(2,1)}) %all-gather.8.cloned.1.call-update) | async-done | bytes 2097168 | tf_op jit(solution)/shard_map/all_gather | solution.py:53
  360.4 10.6 %fusion.1 = f32[512,2048]{1,0:T(8,128)} fusion(bf16[512,2048]{0,1:T(8,128)(2,1)} %all-gather.8.cloned.1.call-done, bf16[2048,2048]{1,0:T(8,128)(2,1)} %all-gather.6.cloned.1.call-done), kind=kOutput, calls=%fused_computation.10 | convolution fusion | flops 4294967296 | bytes 14680064 | tf_op jit(solution)/shard_map/dot_general | solution.py:56
  371.6 3.1 broadcast_in_dim.33
  374.7 10.5 %reshape.42 = pred[512,2048]{1,0:T(8,128)(4,1)S(1)} reshape(pred[16,32,64,32]{3,2,1,0:T(8,128)(4,1)} %broadcast_in_dim.33) | data formatting | bytes 2097152 | tf_op jit(solution)/shard_map/reshape | solution.py:14
  385.2 35.3 %reduce-scatter.2.cloned.1.call-done = f32[512,512]{1,0:T(8,128)} async-done(((f32[512,2048]{1,0:T(8,128)}), f32[512,512]{1,0:T(8,128)}) %reduce-scatter.2.cloned.1.call-update) | async-done | bytes 1048592 | tf_op jit(solution)/shard_map/reduce_scatter | solution.py:57
  420.5 2.3 subtract_convert_fusion
  (16 shorter events, 2.6 us)
Async XLA Ops:
  6.5 57.8 %all-gather.4.cloned.1.call-start = ((), (), s32[]{:S(2)}) async-start(), calls=%async_computation.1 | async-start | bytes 2621440 | tf_op jit(solution)/shard_map/all_gather | solution.py:43
  27.0 95.6 %all-gather.6.cloned.1.call-start = ((), (), s32[]{:S(2)}) async-start(), calls=%async_computation.2 | async-start | bytes 8912896 | tf_op jit(solution)/shard_map/all_gather | solution.py:46
  27.9 332.5 %all-gather.8.cloned.1.call-start = ((), (), s32[]{:S(2)}) async-start(), calls=%async_computation.3 | async-start | bytes 2621440 | tf_op jit(solution)/shard_map/all_gather | solution.py:53
  130.2 97.4 %copy-start = (s32[16,64]{1,0:T(8,128)S(1)}, s32[16,64]{1,0:T(8,128)}, u32[]{:S(2)}) copy-start(s32[16,64]{1,0:T(8,128)} %param.6) | copy-start | bytes 12292
  130.2 92.0 %collective-permute-start = (f32[512,2048]{1,0:T(8,128)S(1)}, f32[512,2048]{1,0:T(8,128)S(1)}, u32[]{:S(2)}, u32[]{:S(2)}) collective-permute-start(f32[512,2048]{1,0:T(8,128)S(1)} %fusion), channel_id=1, source_target_pairs={{0,1},{1,0},{2,3},{3,2},{4,5},{5,4},{6,7},{7,6},{8,9},{9,8},{10,11... | collective-permute-start | bytes 12582920 | tf_op jit(solution)/shard_map/ppermute | solution.py:51
  224.9 92.8 %collective-permute-start.1 = (f32[512,2048]{1,0:T(8,128)}, f32[512,2048]{1,0:T(8,128)}, u32[]{:S(2)}, u32[]{:S(2)}) collective-permute-start(f32[512,2048]{1,0:T(8,128)} %add.20), channel_id=1, source_target_pairs={{0,2},{1,3},{2,0},{3,1},{4,6},{5,7},{6,4},{7,5},{8,10},{9,11},{10,... | collective-permute-start | bytes 12582920 | tf_op jit(solution)/shard_map/ppermute | solution.py:51
  326.9 93.6 %reduce-scatter.2.cloned.1.call-start = ((), (), s32[]{:S(2)}) async-start(), calls=%async_computation.4 | async-start | bytes 5242880 | tf_op jit(solution)/shard_map/reduce_scatter | solution.py:57
  370.9 0.7 copy-start.1
Sparse Core Ops, SparseCore 0:
  27.1 37.2 all-gather.3
  66.2 56.3 all-gather.5
  327.1 33.2 all-gather.7
  371.1 49.3 reduce-scatter.1
